TPU v7x, 32 devices: a whole 2x2x4 slice. The times are simulated.
32 devices in a mesh: rep: 2 (over y), dp: 16 (over z, x, core).
Axes of the slice: x: 2, y: 2, z: 4, core: 2. Of those that a mesh axis runs over, the one named last changes fastest.
Arguments:
- x_copy: bfloat16 [32, 1024, 512], P(('rep', 'dp')), may hold values from -6 to 6
- target_embed: bfloat16 [32, 1024, 512], P(('rep', 'dp')), may hold values from -6 to 6
- memory: bfloat16 [32, 1024, 512], P(('rep', 'dp')), may hold values from -6 to 6
- cotangent: bfloat16 [32, 1024, 512], P(('rep', 'dp')), may hold values from -6 to 6
- segment_ids: int32 [32, 1024], P(('rep', 'dp')), may hold values from 0 to 7, never falling along the last dimension, each value on 1 to 256 neighbouring positions
- source_lengths: int32 [32], P(('rep', 'dp')), may hold values from 256 to 1024
- target_lengths: int32 [32], P(('rep', 'dp')), may hold values from 384 to 1024, as said below
- hamming: int32 [32, 8], P(('rep', 'dp')), may hold values from 0 to 256
- priority: int32 [32, 1024], P(('rep', 'dp')), may hold values from 0 to 1048575
- lang_tag: int32 [32], P(('rep', 'dp')), may hold values from 0 to 63
- w_self_qkv: bfloat16 [3, 512, 512], P(None, None, 'dp'), may hold values from -0.25 to 0.25
- w_self_out: bfloat16 [512, 512], P(None, 'dp'), may hold values from -0.75 to 0.75
- w_cross_q: bfloat16 [512, 512], P(None, 'dp'), may hold values from -0.25 to 0.25
- w_cross_kv: bfloat16 [2, 512, 512], P(None, None, 'dp'), may hold values from -0.25 to 0.25
- w_cross_out: bfloat16 [512, 512], P(None, 'dp'), may hold values from -1 to 1
- w_in: bfloat16 [512, 2048], P(None, 'dp'), may hold values from -0.25 to 0.25
- w_out: bfloat16 [2048, 512], P(None, 'dp'), may hold values from -0.125 to 0.125
- biases: bfloat16 [10, 512], P(None, 'dp'), may hold values from -3 to 3
- gains: bfloat16 [3, 512], P(None, 'dp'), may hold values from 0.25 to 1.75
- b_hidden: bfloat16 [2048], P('dp'), may hold values from -3 to 3
- lang_table: bfloat16 [64, 512], P(None, 'dp'), may hold values from -4 to 4
Outputs:
- first_pass: bfloat16 [32, 1024, 512], P(('rep', 'dp'))
- output: bfloat16 [32, 1024, 512], P(('rep', 'dp'))
- input_grad: float32 [32, 1024, 512], P(('rep', 'dp'))
- memory_grad: float32 [32, 1024, 512], P(('rep', 'dp'))
- grad_self_qkv: float32 [3, 512, 512], P(None, None, 'dp')
- grad_self_out: float32 [512, 512], P(None, 'dp')
- grad_cross_q: float32 [512, 512], P(None, 'dp')
- grad_cross_kv: float32 [2, 512, 512], P(None, None, 'dp')
- grad_cross_out: float32 [512, 512], P(None, 'dp')
- grad_w_in: float32 [512, 2048], P(None, 'dp')
- grad_w_out: float32 [2048, 512], P(None, 'dp')
- grad_biases: float32 [10, 512], P(None, 'dp')
- grad_gains: float32 [3, 512], P(None, 'dp')
- grad_b_hidden: float32 [2048], P('dp')
- grad_lang_table: float32 [64, 512], P(None, 'dp')
Inputs may be any that keep to these rules, and one draw needn't show every extreme that they name: `segment_ids`: segment numbers never fall along a row; each segment holds 1 to 256 token slots. `target_lengths`: some row is full and some row holds the fewest live tokens.
All inputs are finite; a program needn't handle non-finite values.
Results may differ from a plain program's by a relative error of at most 0.024.
The roundings to bfloat16 on the way count: a program that leaves them out, or rounds other values in their place, can miss the bound.
Values may be sent and summed in bfloat16 or wider, within the bound.
A program may use at most 320 MiB of HBM per device.

v0:
```python
from functools import partial

import jax
import jax.numpy as jnp
from jax import lax
from jax.sharding import PartitionSpec as P

HEADS = 8
HD = 64


EPSILON = 1e-05
MASKED = -1000000000.0


def for_sending(shard):

    def short(part):
        return part.astype(jnp.bfloat16) if part.dtype == jnp.float32 else part

    return jax.tree.map(short, shard)


def narrow(value):
    return value.astype(jnp.bfloat16)


def product(left, right):
    return jnp.dot(left, right, preferred_element_type=jnp.float32)


def left_product(left, right):
    return lax.dot_general(
        left, right, (((0,), (0,)), ((), ())), preferred_element_type=jnp.float32
    )


def right_product(left, right):
    return lax.dot_general(
        left, right, (((1,), (1,)), ((), ())), preferred_element_type=jnp.float32
    )


def column_sum(value):
    return jnp.sum(value, axis=0, dtype=jnp.float32)


def layer_norm(value, gain_row, shift_row):
    average = jnp.mean(value, axis=-1, keepdims=True)
    centred = value - average
    variance = jnp.mean(centred * centred, axis=-1, keepdims=True)
    return centred * lax.rsqrt(variance + EPSILON) * gain_row + shift_row


def split_heads(value):
    return value.reshape(value.shape[0], HEADS, HD)


def live_tokens(raw_segments, target_len, doc_slots):
    live = jnp.arange(raw_segments.shape[0], dtype=jnp.int32) < target_len
    segments = jnp.where(live, raw_segments, jnp.int32(doc_slots)).astype(jnp.int32)
    return (live, segments)


def select_glance(segments, hamming_row, priority_row):
    length = segments.shape[0]
    same_doc = segments[:, None] == segments[None, :]
    doc_length = jnp.sum(same_doc.astype(jnp.int32), axis=1)
    slots = jnp.arange(hamming_row.shape[0], dtype=jnp.int32)
    wanted = jnp.sum(
        jnp.where(segments[:, None] == slots[None, :], hamming_row[None, :], 0), axis=1
    )
    glance_count = (jnp.minimum(wanted, doc_length) + 1) // 2
    position = jnp.arange(length, dtype=jnp.int32)
    ranked_ahead = (priority_row[None, :] > priority_row[:, None]) | (
        priority_row[None, :] == priority_row[:, None]
    ) & (position[None, :] < position[:, None])
    rank_in_doc = jnp.sum((same_doc & ranked_ahead).astype(jnp.int32), axis=1)
    return rank_in_doc < glance_count


def attend(queries, key_rows, value_rows, allowed, scaling):
    length = queries.shape[0]
    block_rows = min(512, length)
    contexts = []
    log_parts = []
    for start_row in range(0, length, block_rows):
        query_part = queries[start_row : start_row + block_rows]
        scores = (
            jnp.einsum("qhe,khe->hqk", query_part, key_rows, preferred_element_type=jnp.float32)
            * scaling
        )
        scores = jnp.where(allowed[start_row : start_row + block_rows][None], scores, MASKED)
        largest = jnp.max(scores, axis=-1, keepdims=True)
        powers = jnp.exp(scores - largest)
        denominator = jnp.sum(powers, axis=-1, keepdims=True)
        attn_probs = narrow(powers / denominator)
        contexts.append(
            jnp.einsum("hqk,khe->qhe", attn_probs, value_rows, preferred_element_type=jnp.float32)
        )
        log_parts.append(largest + jnp.log(denominator))
    return (jnp.concatenate(contexts, 0), jnp.concatenate(log_parts, 1))


def attend_back(queries, key_rows, value_rows, allowed, scaling, log_sums, grad_context):
    length = queries.shape[0]
    block_rows = min(512, length)
    grad_keys = jnp.zeros(key_rows.shape, jnp.float32)
    grad_values = jnp.zeros(value_rows.shape, jnp.float32)
    grad_queries = []
    for start_row in range(0, length, block_rows):
        query_part = queries[start_row : start_row + block_rows]
        grad_part = grad_context[start_row : start_row + block_rows]
        scores = (
            jnp.einsum("qhe,khe->hqk", query_part, key_rows, preferred_element_type=jnp.float32)
            * scaling
        )
        scores = jnp.where(allowed[start_row : start_row + block_rows][None], scores, MASKED)
        attn_probs = jnp.exp(scores - log_sums[:, start_row : start_row + block_rows])
        grad_probs = jnp.einsum(
            "qhe,khe->hqk", grad_part, value_rows, preferred_element_type=jnp.float32
        )
        row_delta = jnp.sum(attn_probs * grad_probs, axis=-1, keepdims=True)
        grad_scores = narrow(attn_probs * (grad_probs - row_delta))
        grad_values = grad_values + jnp.einsum(
            "hqk,qhe->khe", narrow(attn_probs), grad_part, preferred_element_type=jnp.float32
        )
        grad_queries.append(
            jnp.einsum("hqk,khe->qhe", grad_scores, key_rows, preferred_element_type=jnp.float32)
            * scaling
        )
        grad_keys = (
            grad_keys
            + jnp.einsum(
                "hqk,qhe->khe", grad_scores, query_part, preferred_element_type=jnp.float32
            )
            * scaling
        )
    return (jnp.concatenate(grad_queries, 0), grad_keys, grad_values)


def forward(inputs, key_cross, value_cross, same_doc, source_mask, weights):
    (
        w_qkv,
        w_self_o,
        w_cross_q,
        w_cross_kv,
        w_cross_o,
        w_up,
        w_down,
        bias_rows,
        gain_rows,
        bias_mid,
    ) = weights
    length = inputs.shape[0]
    scaling = HD ** (-0.5)
    low_in = narrow(inputs)
    queries = narrow(product(low_in, w_qkv[0]) + bias_rows[0])
    key_self = narrow(product(low_in, w_qkv[1]))
    value_self = narrow(product(low_in, w_qkv[2]) + bias_rows[1])
    context, log_sums = attend(
        split_heads(queries), split_heads(key_self), split_heads(value_self), same_doc, scaling
    )
    ctx_low = narrow(context.reshape(length, -1))
    first_sum = inputs + product(ctx_low, w_self_o) + bias_rows[2]
    after_self = layer_norm(first_sum, gain_rows[0], bias_rows[7])
    low_self = narrow(after_self)
    cross_queries = narrow(product(low_self, w_cross_q) + bias_rows[3])
    context_two, log_sums_two = attend(
        split_heads(cross_queries),
        split_heads(key_cross),
        split_heads(value_cross),
        source_mask,
        scaling,
    )
    ctx_two_low = narrow(context_two.reshape(length, -1))
    second_sum = after_self + product(ctx_two_low, w_cross_o) + bias_rows[5]
    after_cross = layer_norm(second_sum, gain_rows[1], bias_rows[8])
    low_cross = narrow(after_cross)
    before_act = product(low_cross, w_up) + bias_mid
    hidden = narrow(jax.nn.gelu(before_act, approximate=False))
    third_sum = after_cross + product(hidden, w_down) + bias_rows[6]
    result = layer_norm(third_sum, gain_rows[2], bias_rows[9])
    saved = (
        low_in,
        queries,
        key_self,
        value_self,
        log_sums,
        ctx_low,
        first_sum,
        low_self,
        cross_queries,
        log_sums_two,
        ctx_two_low,
        second_sum,
        low_cross,
        before_act,
        hidden,
        third_sum,
    )
    return (result, saved)


def backward(saved, grad_out, key_cross, value_cross, memory_row, same_doc, source_mask, weights):
    (
        w_qkv,
        w_self_o,
        w_cross_q,
        w_cross_kv,
        w_cross_o,
        w_up,
        w_down,
        bias_rows,
        gain_rows,
        bias_mid,
    ) = weights
    (
        low_in,
        queries,
        key_self,
        value_self,
        log_sums,
        ctx_low,
        first_sum,
        low_self,
        cross_queries,
        log_sums_two,
        ctx_two_low,
        second_sum,
        low_cross,
        before_act,
        hidden,
        third_sum,
    ) = saved
    length = low_in.shape[0]
    scaling = HD ** (-0.5)
    gain_float = gain_rows.astype(jnp.float32)
    shift_float = bias_rows.astype(jnp.float32)

    def norm_back(total_in, index, grad_norm):
        unused, pull = jax.vjp(layer_norm, total_in, gain_float[index], shift_float[7 + index])
        return pull(grad_norm)

    grad_third, g_gain_three, g_shift_three = norm_back(third_sum, 2, grad_out)
    grad_ffn = narrow(grad_third)
    g_b_down = column_sum(grad_ffn)
    g_w_down = left_product(hidden, grad_ffn)
    grad_hidden = right_product(grad_ffn, w_down)
    unused, pull_gelu = jax.vjp(partial(jax.nn.gelu, approximate=False), before_act)
    grad_pre = narrow(pull_gelu(grad_hidden)[0])
    g_b_mid = column_sum(grad_pre)
    g_w_up = left_product(low_cross, grad_pre)
    grad_cross_out = grad_third + right_product(grad_pre, w_up)
    grad_second, g_gain_two, g_shift_two = norm_back(second_sum, 1, grad_cross_out)
    grad_branch_two = narrow(grad_second)
    g_b_cross_o = column_sum(grad_branch_two)
    g_w_cross_o = left_product(ctx_two_low, grad_branch_two)
    grad_ctx_two = narrow(right_product(grad_branch_two, w_cross_o))
    gq_two, gk_two, gv_two = attend_back(
        split_heads(cross_queries),
        split_heads(key_cross),
        split_heads(value_cross),
        source_mask,
        scaling,
        log_sums_two,
        split_heads(grad_ctx_two),
    )
    gq_two = narrow(gq_two.reshape(length, -1))
    gk_two = narrow(gk_two.reshape(key_cross.shape[0], -1))
    gv_two = narrow(gv_two.reshape(value_cross.shape[0], -1))
    g_w_cross_q = left_product(low_self, gq_two)
    g_w_cross_kv = jnp.stack([left_product(memory_row, gk_two), left_product(memory_row, gv_two)])
    grad_memory = right_product(gk_two, w_cross_kv[0]) + right_product(gv_two, w_cross_kv[1])
    grad_self_out = grad_second + right_product(gq_two, w_cross_q)
    grad_first, g_gain_one, g_shift_one = norm_back(first_sum, 0, grad_self_out)
    grad_branch = narrow(grad_first)
    g_b_self_o = column_sum(grad_branch)
    g_w_self_o = left_product(ctx_low, grad_branch)
    grad_ctx = narrow(right_product(grad_branch, w_self_o))
    gq_one, gk_one, gv_one = attend_back(
        split_heads(queries),
        split_heads(key_self),
        split_heads(value_self),
        same_doc,
        scaling,
        log_sums,
        split_heads(grad_ctx),
    )
    gq_one = narrow(gq_one.reshape(length, -1))
    gk_one = narrow(gk_one.reshape(length, -1))
    gv_one = narrow(gv_one.reshape(length, -1))
    g_w_qkv = jnp.stack(
        [left_product(low_in, gq_one), left_product(low_in, gk_one), left_product(low_in, gv_one)]
    )
    grad_input = (
        grad_first
        + right_product(gq_one, w_qkv[0])
        + right_product(gk_one, w_qkv[1])
        + right_product(gv_one, w_qkv[2])
    )
    g_bias = jnp.stack(
        [
            column_sum(gq_one),
            column_sum(gv_one),
            g_b_self_o,
            column_sum(gq_two),
            column_sum(gv_two),
            g_b_cross_o,
            g_b_down,
            g_shift_one,
            g_shift_two,
            g_shift_three,
        ]
    )
    g_gain = jnp.stack([g_gain_one, g_gain_two, g_gain_three])
    gradients = (
        g_w_qkv,
        g_w_self_o,
        g_w_cross_q,
        g_w_cross_kv,
        g_w_cross_o,
        g_w_up,
        g_w_down,
        g_bias,
        g_gain,
        g_b_mid,
    )
    return (grad_input, grad_memory, gradients)


def shards(
    x_copy,
    target_embed,
    memory,
    cotangent,
    segment_ids,
    source_lengths,
    target_lengths,
    hamming,
    priority,
    lang_tag,
    w_self_qkv,
    w_self_out,
    w_cross_q,
    w_cross_kv,
    w_cross_out,
    w_in,
    w_out,
    biases,
    gains,
    b_hidden,
    lang_table,
):
    whole = (
        lax.all_gather(w_self_qkv, "dp", axis=2, tiled=True),
        lax.all_gather(w_self_out, "dp", axis=1, tiled=True),
        lax.all_gather(w_cross_q, "dp", axis=1, tiled=True),
        lax.all_gather(w_cross_kv, "dp", axis=2, tiled=True),
        lax.all_gather(w_cross_out, "dp", axis=1, tiled=True),
        lax.all_gather(w_in, "dp", axis=1, tiled=True),
        lax.all_gather(w_out, "dp", axis=1, tiled=True),
        lax.all_gather(biases, "dp", axis=1, tiled=True),
        lax.all_gather(gains, "dp", axis=1, tiled=True),
        lax.all_gather(b_hidden, "dp", axis=0, tiled=True),
        lax.all_gather(lang_table, "dp", axis=1, tiled=True),
    )
    layer_weights = whole[:10]
    lang_whole = whole[10]
    lang_count = lang_whole.shape[0]
    source_count = memory.shape[1]
    doc_slots = hamming.shape[1]

    def masks(segments, source_len):
        same_doc = segments[:, None] == segments[None, :]
        source_mask = jnp.broadcast_to(
            jnp.arange(source_count, dtype=jnp.int32)[None, :] < source_len,
            (segments.shape[0], source_count),
        )
        return (same_doc, source_mask)

    def forward_row(row_data):
        (
            copy_row,
            target_row,
            memory_row,
            raw_segments,
            source_len,
            target_len,
            hamming_row,
            priority_row,
            language,
        ) = row_data
        live, segments = live_tokens(raw_segments, target_len, doc_slots)
        same_doc, source_mask = masks(segments, source_len)
        one_hot = (jnp.arange(lang_count, dtype=jnp.int32) == language).astype(jnp.bfloat16)
        lang_vector = product(one_hot[None, :], lang_whole)
        copy_float = copy_row.astype(jnp.float32)
        target_float = target_row.astype(jnp.float32)
        glance = select_glance(segments, hamming_row, priority_row)
        key_cross = narrow(product(memory_row, layer_weights[3][0]))
        value_cross = narrow(product(memory_row, layer_weights[3][1]) + layer_weights[7][4])
        first_out, unused = forward(
            copy_float + lang_vector, key_cross, value_cross, same_doc, source_mask, layer_weights
        )
        mixed = jnp.where(glance[:, None], target_float, copy_float) + lang_vector
        final_out, saved = forward(
            mixed, key_cross, value_cross, same_doc, source_mask, layer_weights
        )
        return (narrow(first_out), narrow(final_out), saved, key_cross, value_cross)

    firsts, finals, saved_all, keys_all, values_all = lax.map(
        forward_row,
        (
            x_copy,
            target_embed,
            memory,
            segment_ids,
            source_lengths,
            target_lengths,
            hamming,
            priority,
            lang_tag,
        ),
    )
    back_weights = (
        lax.all_gather(w_self_qkv, "dp", axis=2, tiled=True),
        lax.all_gather(w_self_out, "dp", axis=1, tiled=True),
        lax.all_gather(w_cross_q, "dp", axis=1, tiled=True),
        lax.all_gather(w_cross_kv, "dp", axis=2, tiled=True),
        lax.all_gather(w_cross_out, "dp", axis=1, tiled=True),
        lax.all_gather(w_in, "dp", axis=1, tiled=True),
        lax.all_gather(w_out, "dp", axis=1, tiled=True),
        lax.all_gather(biases, "dp", axis=1, tiled=True),
        lax.all_gather(gains, "dp", axis=1, tiled=True),
        lax.all_gather(b_hidden, "dp", axis=0, tiled=True),
    )

    def backward_row(totals, row_data):
        (
            saved_row,
            key_cross,
            value_cross,
            memory_row,
            grad_rows,
            raw_segments,
            source_len,
            target_len,
            language,
        ) = row_data
        live, segments = live_tokens(raw_segments, target_len, doc_slots)
        same_doc, source_mask = masks(segments, source_len)
        live_grad = grad_rows.astype(jnp.float32) * live[:, None].astype(jnp.float32)
        grad_input, grad_memory, gradients = backward(
            saved_row,
            live_grad,
            key_cross,
            value_cross,
            memory_row,
            same_doc,
            source_mask,
            back_weights,
        )
        one_hot = (jnp.arange(lang_count, dtype=jnp.int32) == language).astype(jnp.float32)
        grad_lang = one_hot[:, None] * jnp.sum(grad_input, axis=0)[None, :]
        totals = jax.tree.map(jnp.add, totals, gradients + (grad_lang,))
        return (totals, (grad_input, grad_memory))

    zero_sums = tuple((jnp.zeros(weight.shape, jnp.float32) for weight in whole))
    local_grads, row_grads = lax.scan(
        backward_row,
        zero_sums,
        (
            saved_all,
            keys_all,
            values_all,
            memory,
            cotangent,
            segment_ids,
            source_lengths,
            target_lengths,
            lang_tag,
        ),
    )
    grad_inputs, grad_memories = row_grads
    owned = (
        lax.psum_scatter(local_grads[0], "dp", scatter_dimension=2, tiled=True),
        lax.psum_scatter(local_grads[1], "dp", scatter_dimension=1, tiled=True),
        lax.psum_scatter(local_grads[2], "dp", scatter_dimension=1, tiled=True),
        lax.psum_scatter(local_grads[3], "dp", scatter_dimension=2, tiled=True),
        lax.psum_scatter(local_grads[4], "dp", scatter_dimension=1, tiled=True),
        lax.psum_scatter(local_grads[5], "dp", scatter_dimension=1, tiled=True),
        lax.psum_scatter(local_grads[6], "dp", scatter_dimension=1, tiled=True),
        lax.psum_scatter(local_grads[7], "dp", scatter_dimension=1, tiled=True),
        lax.psum_scatter(local_grads[8], "dp", scatter_dimension=1, tiled=True),
        lax.psum_scatter(local_grads[9], "dp", scatter_dimension=0, tiled=True),
        lax.psum_scatter(local_grads[10], "dp", scatter_dimension=1, tiled=True),
    )
    shares = jax.tree.map(
        lambda part: part.astype(jnp.float32), lax.psum(for_sending(owned), "rep")
    )
    (
        g_qkv,
        g_self_o,
        g_cross_q,
        g_cross_kv,
        g_cross_o,
        g_up,
        g_down,
        g_bias,
        g_gain,
        g_mid,
        g_lang,
    ) = shares
    return (
        firsts,
        finals,
        grad_inputs,
        grad_memories,
        g_qkv,
        g_self_o,
        g_cross_q,
        g_cross_kv,
        g_cross_o,
        g_up,
        g_down,
        g_bias,
        g_gain,
        g_mid,
        g_lang,
    )


def solution(mesh):
    placed = (
        P(("rep", "dp"), None, None),
        P(("rep", "dp"), None, None),
        P(("rep", "dp"), None, None),
        P(("rep", "dp"), None, None),
        P(("rep", "dp"), None),
        P(("rep", "dp")),
        P(("rep", "dp")),
        P(("rep", "dp"), None),
        P(("rep", "dp"), None),
        P(("rep", "dp")),
        P(None, None, "dp"),
        P(None, "dp"),
        P(None, "dp"),
        P(None, None, "dp"),
        P(None, "dp"),
        P(None, "dp"),
        P(None, "dp"),
        P(None, "dp"),
        P(None, "dp"),
        P("dp"),
        P(None, "dp"),
    )
    return jax.shard_map(
        shards,
        mesh=mesh,
        in_specs=placed,
        out_specs=(
            P(("rep", "dp"), None, None),
            P(("rep", "dp"), None, None),
            P(("rep", "dp"), None, None),
            P(("rep", "dp"), None, None),
            P(None, None, "dp"),
            P(None, "dp"),
            P(None, "dp"),
            P(None, None, "dp"),
            P(None, "dp"),
            P(None, "dp"),
            P(None, "dp"),
            P(None, "dp"),
            P(None, "dp"),
            P("dp"),
            P(None, "dp"),
        ),
        check_vma=False,
    )
```

profile of v0, /device:TPU:0, one launch (start us, length us, event | category | flops | bytes accessed | tf_op | source)
XLA Modules:
  0.0 1205.7 jit_solution(2309971384177394625)
XLA Ops:
  13.1 23.1 %all-gather.2 = bf16[16,1,128]{2,1,0:T(2,128)(2,1)S(1)} all-gather(bf16[1,1,128]{2,1,0:T(2,128)(2,1)} %bitcast.475), channel_id=1, replica_groups=mesh['rep'=2,'dp'=16] {'dp'}, dimensions={0}, use_global_device_ids=true | all-gather | bytes 4352 | tf_op jit(solution)/shard_map/all_gather | solution.py:365
  42.6 17.7 %all-gather.1 = bf16[16,32,3]{1,2,0:T(4,128)(2,1)S(1)} all-gather(bf16[1,32,3]{1,2,0:T(4,128)(2,1)} %bitcast.474), channel_id=1, replica_groups=mesh['rep'=2,'dp'=16] {'dp'}, dimensions={0}, use_global_device_ids=true | all-gather | bytes 3264 | tf_op jit(solution)/shard_map/all_gather | solution.py:364
  61.5 19.3 %all-gather = bf16[16,32,10]{1,2,0:T(8,128)(2,1)S(1)} all-gather(bf16[1,32,10]{1,2,0:T(8,128)(2,1)} %bitcast.440), channel_id=1, replica_groups=mesh['rep'=2,'dp'=16] {'dp'}, dimensions={0}, use_global_device_ids=true | all-gather | bytes 10880 | tf_op jit(solution)/shard_map/all_gather | solution.py:363
  81.5 18.0 %all_gather.41 = bf16[64,512]{0,1:T(8,128)(2,1)S(1)} all-gather(bf16[64,32]{0,1:T(8,128)(2,1)} %param.41), channel_id=1, replica_groups=mesh['rep'=2,'dp'=16] {'dp'}, dimensions={1}, use_global_device_ids=true | all-gather | bytes 69632 | tf_op jit(solution)/shard_map/all_gather | solution.py:366
  99.6 22.3 %all_gather.44 = bf16[512,512]{0,1:T(8,128)(2,1)} all-gather(bf16[512,32]{0,1:T(8,128)(2,1)} %param.32), channel_id=1, replica_groups=mesh['rep'=2,'dp'=16] {'dp'}, dimensions={1}, use_global_device_ids=true | all-gather | bytes 557056 | tf_op jit(solution)/shard_map/all_gather | solution.py:357
  121.8 20.9 %all_gather.47 = bf16[512,512]{0,1:T(8,128)(2,1)} all-gather(bf16[512,32]{0,1:T(8,128)(2,1)} %param.33), channel_id=1, replica_groups=mesh['rep'=2,'dp'=16] {'dp'}, dimensions={1}, use_global_device_ids=true | all-gather | bytes 557056 | tf_op jit(solution)/shard_map/all_gather | solution.py:358
  142.7 23.4 %all_gather.48 = bf16[512,512]{0,1:T(8,128)(2,1)} all-gather(bf16[512,32]{0,1:T(8,128)(2,1)} %param.35), channel_id=1, replica_groups=mesh['rep'=2,'dp'=16] {'dp'}, dimensions={1}, use_global_device_ids=true | all-gather | bytes 557056 | tf_op jit(solution)/shard_map/all_gather | solution.py:360
  185.9 10.6 fusion.239
  196.5 10.8 fusion.238
  302.5 13.6 %fusion.7 = f32[8,512]{1,0:T(8,128)S(1)} fusion(f32[8,512,1024]{2,1,0:T(8,128)} %get-tuple-element.417, f32[8,512]{1,0:T(8,128)S(1)} %get-tuple-element.416), kind=kLoop, calls=%fused_computation.43 | loop fusion | flops 8384512 | bytes 16809984 | tf_op jit(solution)/shard_map/while/body/eval_jaxpr/reduce_sum | solution.py:96
  355.2 27.0 %fusion.244 = (f32[1024]{0:T(1024)S(1)}, f32[1024,512]{0,1:T(8,128)}) fusion(f32[512]{0:T(512)S(1)} %bitcast.450, bf16[2048,512]{0,1:T(8,128)(2,1)} %all-gather.14.cloned.1.call-done, f32[2048]{0:T(1024)S(1)} %bitcast.428, bf16[512,2048]{1,0:T(8,128)(2,1)} %all-gather.12.cloned.1.call-done, f32[1024,512]{0,1:T(8,128)} %copy-done.55, f32[512]{0:T(512)S(1)} %bitcast.441, ...), kind=kOutput, calls=%fused_computation.406 | convolution fusion | flops 4439669760 | bytes 8415232 | tf_op jit(solution)/shard_map/while/body/eval_jaxpr/dot_general | solution.py:29
  382.2 23.9 %multiply_convert_fusion.4 = (bf16[1024,2048]{1,0:T(8,128)(2,1)S(1)}, f32[1024,2048]{1,0:T(8,128)S(1)}, f32[1024,2048]{1,0:T(8,128)}) fusion(f32[2048]{0:T(1024)S(1)} %bitcast.429, bf16[512,2048]{1,0:T(8,128)(2,1)} %all-gather.12.cloned.1.call-done, f32[1024,512]{0,1:T(8,128)S(1)} %get-tuple-element.421, f32[1024]{0:T(1024)S(1)} %fusion.154, ...), kind=kOutput, calls=%fused_computation.68 | convolution fusion | flops 2288517120 | bytes 25186304 | tf_op jit(solution)/shard_map/while/body/eval_jaxpr/dot_general | solution.py:29
  440.0 13.2 %multiply_reduce_fusion.2 = (f32[8,512]{1,0:T(8,128)S(1)}, f32[8,512,1024]{2,1,0:T(8,128)}) fusion(f32[8,512,1024]{2,1,0:T(8,128)} %get-tuple-element.417, f32[8,512]{1,0:T(8,128)S(1)} %log_add_fusion.2, bf16[512,8,64]{0,2,1:T(8,128)(2,1)S(1)} %bitcast.371, bf16[1024,8,64]{0,2,1:T(8,128)(2,1)} %bitcast.372), kind=kOutput, calls=%fused_computation.11 | convolution fusion | flops 549449728 | bytes 35160064 | tf_op jit(solution)/shard_map/while/body/eval_jaxpr/qhe,khe->hqk/dot_general | solution.py:120
  462.6 10.5 multiply_convert_fusion.3
  479.2 12.0 multiply_convert_fusion.2
  512.2 16.1 %multiply_convert_fusion.1 = bf16[8,512,1024]{2,1,0:T(8,128)(2,1)} fusion(f32[8,512,1024]{2,1,0:T(8,128)} %get-tuple-element.446, f32[8,512,1024]{2,1,0:T(8,128)} %get-tuple-element.413, f32[8,512]{1,0:T(8,128)} %get-tuple-element.445, f32[8,512]{1,0:T(8,128)S(1)} %copy-done.76), kind=kLoop, calls=%fused_computation.7 | loop fusion | flops 16777216 | bytes 41975808 | tf_op jit(solution)/shard_map/while/body/eval_jaxpr/convert_element_type | solution.py:25
  656.3 101.4 %all-reduce.12 = (bf16[3,512,512]{1,0,2:T(4,128)(2,1)S(1)}, bf16[2048]{0:T(1024)(128)(2,1)S(1)}) all-reduce(f32[3,512,512]{1,0,2:T(4,128)} %copy.91, f32[2048]{0:T(1024)S(1)} %copy-done.97), channel_id=2, replica_groups=mesh['rep'=2,'dp'=16] {'dp'}, use_global_device_ids=true, to_apply=%region_41.42.clone | all-reduce | flops 788480 | bytes 4730880
  762.4 36.8 %reduce-scatter.20.cloned.1.call-done = f32[512,32]{0,1:T(8,128)} async-done(((f32[512,512]{0,1:T(8,128)}), f32[512,32]{0,1:T(8,128)}) %reduce-scatter.20.cloned.1.call-update) | async-done | bytes 65552 | tf_op jit(solution)/shard_map/reduce_scatter | solution.py:491
  800.6 59.1 %reduce-scatter.16.cloned.1.call-done = f32[512,32]{0,1:T(8,128)} async-done(((f32[512,512]{0,1:T(8,128)}), f32[512,32]{0,1:T(8,128)}) %reduce-scatter.16.cloned.1.call-update) | async-done | bytes 65552 | tf_op jit(solution)/shard_map/reduce_scatter | solution.py:489
  861.2 58.5 %reduce-scatter.14.cloned.1.call-done = f32[512,32]{0,1:T(8,128)} async-done(((f32[512,512]{0,1:T(8,128)}), f32[512,32]{0,1:T(8,128)}) %reduce-scatter.14.cloned.1.call-update) | async-done | bytes 65552 | tf_op jit(solution)/shard_map/reduce_scatter | solution.py:488
  922.2 62.9 %reduce-scatter.18.cloned.1.call-done = f32[2,512,32]{1,2,0:T(8,128)} async-done(((f32[2,512,512]{1,2,0:T(8,128)}), f32[2,512,32]{1,2,0:T(8,128)}) %reduce-scatter.18.cloned.1.call-update) | async-done | bytes 131088 | tf_op jit(solution)/shard_map/reduce_scatter | solution.py:490
  986.7 73.6 %reduce-scatter.24.cloned.1.call-done = f32[2048,32]{0,1:T(8,128)} async-done(((f32[2048,512]{0,1:T(8,128)}), f32[2048,32]{0,1:T(8,128)}) %reduce-scatter.24.cloned.1.call-update) | async-done | bytes 262160 | tf_op jit(solution)/shard_map/reduce_scatter | solution.py:493
  1061.9 74.5 %reduce-scatter.22.cloned.1.call-done = f32[512,128]{1,0:T(8,128)} async-done(((f32[512,2048]{1,0:T(8,128)}), f32[512,128]{1,0:T(8,128)}) %reduce-scatter.22.cloned.1.call-update) | async-done | bytes 262160 | tf_op jit(solution)/shard_map/reduce_scatter | solution.py:492
  1170.5 22.0 %all-reduce.11.cloned.1.call-done = (bf16[3,512,32]{1,0,2:T(4,128)(2,1)}, bf16[2,512,32]{1,2,0:T(8,128)(2,1)}, bf16[512,128]{1,0:T(8,128)(2,1)}, bf16[2048,32]{0,1:T(8,128)(2,1)}) async-done(((bf16[3,512,32]{1,0,2:T(4,128)(2,1)}, bf16[2,512,32]{1,2,0:T(8,128)(2,1)}, bf16[512,128]{1,0:T(8,128)(2,1)}, bf16[2048,32]{0,1:T(8,128)(2,1)}), (bf16[3,512,32]{1,0,2:T(4,128)(2,1)}, bf16[2,512,32]{1,2,0:T(8,128)(2,1)}, ...) | async-done | bytes 426000 | tf_op jit(solution)/shard_map/psum | solution.py:500
  (497 shorter events, 415.3 us)
Async XLA Ops:
  7.2 166.1 %copy-start = (bf16[1,1024,512]{2,1,0:T(8,128)(2,1)S(1)}, bf16[1,1024,512]{2,1,0:T(8,128)(2,1)}, u32[]{:S(2)}) copy-start(bf16[1,1024,512]{2,1,0:T(8,128)(2,1)} %param.23) | copy-start | bytes 3145732
  7.2 159.9 %copy-start.61 = (bf16[1,1024,512]{2,1,0:T(8,128)(2,1)S(1)}, bf16[1,1024,512]{2,1,0:T(8,128)(2,1)}, u32[]{:S(2)}) copy-start(bf16[1,1024,512]{2,1,0:T(8,128)(2,1)} %param.21) | copy-start | bytes 3145732
  7.2 166.1 %all-gather.10.cloned.1.call-start = ((), (), s32[]{:S(2)}) async-start(), calls=%async_computation.10 | async-start | bytes 1114112 | tf_op jit(solution)/shard_map/all_gather | solution.py:359
  7.9 170.3 %all-gather.8.cloned.1.call-start = ((), (), s32[]{:S(2)}) async-start(), calls=%async_computation.9 | async-start | bytes 1671168 | tf_op jit(solution)/shard_map/all_gather | solution.py:356
  8.7 346.5 %all-gather.12.cloned.1.call-start = ((), (), s32[]{:S(2)}) async-start(), calls=%async_computation.11 | async-start | bytes 2228224 | tf_op jit(solution)/shard_map/all_gather | solution.py:361
  9.4 345.7 %all-gather.14.cloned.1.call-start = ((), (), s32[]{:S(2)}) async-start(), calls=%async_computation.12 | async-start | bytes 2228224 | tf_op jit(solution)/shard_map/all_gather | solution.py:362
  10.0 748.4 %reduce-scatter.30.cloned.1.call-start = ((), (), s32[]{:S(2)}) async-start(), calls=%async_computation.21 | async-start | bytes 278528
  60.9 290.8 %copy-start.120 = (f32[1,512]{1,0:T(1,128)}, f32[1,512]{1,0:T(1,128)S(1)}, u32[]{:S(2)}) copy-start(f32[1,512]{1,0:T(1,128)S(1)} %get-tuple-element.409) | copy-start | bytes 6148
  81.5 270.2 %copy-start.113 = (f32[1,512]{1,0:T(1,128)}, f32[1,512]{1,0:T(1,128)S(1)}, u32[]{:S(2)}) copy-start(f32[1,512]{1,0:T(1,128)S(1)} %get-tuple-element.397) | copy-start | bytes 6148
  175.0 124.9 %copy-start.15 = (bf16[1024,512]{0,1:T(8,128)(2,1)}, bf16[1024,512]{0,1:T(8,128)(2,1)S(1)}, u32[]{:S(2)}) copy-start(bf16[1024,512]{0,1:T(8,128)(2,1)S(1)} %convolution_convert_fusion.4) | copy-start | bytes 3145732
  180.6 75.9 %copy-start.30 = (bf16[512,512]{0,1:T(8,128)(2,1)}, bf16[512,512]{0,1:T(8,128)(2,1)S(1)}, u32[]{:S(2)}) copy-start(bf16[512,512]{0,1:T(8,128)(2,1)S(1)} %get-tuple-element.383) | copy-start | bytes 1572868
  352.7 75.8 %copy-start.19 = (f32[1024,512]{0,1:T(8,128)}, f32[1024,512]{0,1:T(8,128)S(1)}, u32[]{:S(2)}) copy-start(f32[1024,512]{0,1:T(8,128)S(1)} %get-tuple-element.421) | copy-start | bytes 6291460
  352.7 75.8 %copy-start.85 = (f32[1024]{0:T(1024)}, f32[1024]{0:T(1024)S(1)}, u32[]{:S(2)}) copy-start(f32[1024]{0:T(1024)S(1)} %broadcast_multiply_fusion.2) | copy-start | bytes 12292
  353.0 75.5 %copy-start.95 = (f32[1024]{0:T(1024)}, f32[1024]{0:T(1024)S(1)}, u32[]{:S(2)}) copy-start(f32[1024]{0:T(1024)S(1)} %fusion.154) | copy-start | bytes 12292
  566.7 193.0 %reduce-scatter.28.cloned.1.call-start = ((), (), s32[]{:S(2)}) async-start(), calls=%async_computation.20 | async-start | bytes 278528
  593.4 167.7 %reduce-scatter.26.cloned.1.call-start = ((), (), s32[]{:S(2)}) async-start(), calls=%async_computation.19 | async-start | bytes 278528 | tf_op jit(solution)/shard_map/reduce_scatter | solution.py:497
  602.0 197.1 %reduce-scatter.20.cloned.1.call-start = ((), (), s32[]{:S(2)}) async-start(), calls=%async_computation.16 | async-start | bytes 1114112 | tf_op jit(solution)/shard_map/reduce_scatter | solution.py:491
  605.4 254.4 %reduce-scatter.16.cloned.1.call-start = ((), (), s32[]{:S(2)}) async-start(), calls=%async_computation.14 | async-start | bytes 1114112 | tf_op jit(solution)/shard_map/reduce_scatter | solution.py:489
  608.6 311.1 %reduce-scatter.14.cloned.1.call-start = ((), (), s32[]{:S(2)}) async-start(), calls=%async_computation.13 | async-start | bytes 1114112 | tf_op jit(solution)/shard_map/reduce_scatter | solution.py:488
  614.7 370.4 %reduce-scatter.18.cloned.1.call-start = ((), (), s32[]{:S(2)}) async-start(), calls=%async_computation.15 | async-start | bytes 2228224 | tf_op jit(solution)/shard_map/reduce_scatter | solution.py:490
  628.1 432.2 %reduce-scatter.24.cloned.1.call-start = ((), (), s32[]{:S(2)}) async-start(), calls=%async_computation.18 | async-start | bytes 4456448 | tf_op jit(solution)/shard_map/reduce_scatter | solution.py:493
  634.7 501.6 %reduce-scatter.22.cloned.1.call-start = ((), (), s32[]{:S(2)}) async-start(), calls=%async_computation.17 | async-start | bytes 4456448 | tf_op jit(solution)/shard_map/reduce_scatter | solution.py:492
  643.0 518.3 %all-reduce.9.cloned.1.call-start = ((), (), s32[]{:S(2)}) async-start(), calls=%async_computation.22 | async-start | bytes 224256 | tf_op jit(solution)/shard_map/psum | solution.py:500
  921.2 271.4 %all-reduce.11.cloned.1.call-start = ((), (), s32[]{:S(2)}) async-start(), calls=%async_computation.23 | async-start | bytes 917504 | tf_op jit(solution)/shard_map/psum | solution.py:500
  (132 other events, 1092.0 us)
Sparse Core Ops, SparseCore 0:
  10.2 40.6 all-gather.9
  53.1 38.7 all-gather.7
  94.1 43.7 all-gather.11
  139.9 40.8 all-gather.13
  566.8 51.8 reduce-scatter.29
  622.6 54.9 reduce-scatter.27
  681.2 56.8 reduce-scatter.25
  741.7 57.4 reduce-scatter.19
  803.2 56.4 reduce-scatter.15
  863.2 56.4 reduce-scatter.13
  924.5 60.6 reduce-scatter.17
  988.8 71.4 reduce-scatter.23
  1064.6 71.7 reduce-scatter.21
  1140.1 21.2 all-reduce.8
  1164.8 27.6 all-reduce.10
where the time goes:
time: 1210 us
  waiting for transfers between devices  399 us (33%)
  matrix products  372 us (31%)
  blocking collectives  246 us (20%)
  other arithmetic  127 us (10%)
  local copies, waits for them, and re-layouts  40.9 us (3%)
  between operations  19.4 us (2%)
    unnamed x1, blocking collectives  101 us
    dot_general x18, matrix products, product(): return jnp.dot(left, right, preferred_element_type=jnp.float32)  76.3 us
    reduce_scatter x1, waiting for transfers between devices, shards(): lax.psum_scatter(local_grads[5], 'dp', scatter_dimension=1, tiled=True)  74.5 us
    reduce_scatter x1, waiting for transfers between devices, shards(): lax.psum_scatter(local_grads[6], 'dp', scatter_dimension=1, tiled=True)  73.6 us
    reduce_scatter x1, waiting for transfers between devices, shards(): lax.psum_scatter(local_grads[3], 'dp', scatter_dimension=2, tiled=True)  62.9 us
    reduce_scatter x1, waiting for transfers between devices, shards(): lax.psum_scatter(local_grads[2], 'dp', scatter_dimension=1, tiled=True)  59.1 us
    reduce_scatter x1, waiting for transfers between devices, shards(): lax.psum_scatter(local_grads[1], 'dp', scatter_dimension=1, tiled=True)  58.5 us
    dot_general x8, matrix products, attend(): jnp.einsum('hqk,khe->qhe', attn_probs, value_rows, preferred_element_type...  57.5 us
  transfers between devices with their start and end apart: 15, of which 8 were waited for; matrix products, arithmetic and copies ran while one was open for 26% of the time, Pallas kernels for 0%

commit v1 on v0

v1 whole, which is shorter than its diff:
```python
import functools
import math

import jax
import jax.numpy as jnp
from jax import lax
from jax.experimental import pallas as pl
from jax.experimental.pallas import tpu as pltpu
from jax.sharding import PartitionSpec as P

f32, bf16 = jnp.float32, jnp.bfloat16
MESH = pl.DeviceIdType.MESH
VMEM = pltpu.VMEM

HEADS = 8
HD = 64
EPSILON = 1e-05
MASKED = -1000000000.0
LOG2E = 1.4426950408889634
SCORE = LOG2E * HD ** (-0.5)
SCALING = HD ** (-0.5)

NT = (((1,), (1,)), ((), ()))
NN = (((1,), (0,)), ((), ()))
TN = (((0,), (0,)), ((), ()))

BIASES, GAINS = 10, 3


def dot(left, right, form):
    return lax.dot_general(left, right, form, preferred_element_type=f32)


def own_bits(index, depth):
    return [lax.rem(index // (1 << (depth - 1 - j)), 2) for j in range(depth)]


def partner_of(index, bit, depth, j):
    return index + (1 - 2 * bit) * (1 << (depth - 1 - j))


def enter(rep, me, partners, with_rep):
    barrier = pltpu.get_barrier_semaphore()
    for partner in partners:
        pl.semaphore_signal(barrier, inc=1, device_id=(rep, partner), device_id_type=MESH)
    if with_rep:
        pl.semaphore_signal(barrier, inc=1, device_id=(1 - rep, me), device_id_type=MESH)
    pl.semaphore_wait(barrier, len(partners) + int(with_rep))


def gather_kernel(depth, pieces, count, *refs):
    ins, outs = refs[:count], refs[count : 2 * count]
    send, recv, local = refs[2 * count :]
    rep, me = lax.axis_index("rep"), lax.axis_index("dp")
    bits = own_bits(me, depth)
    partners = [partner_of(me, bits[j], depth, j) for j in range(depth)]
    copies = [
        pltpu.make_async_copy(ins[i], outs[i].at[tuple(bits)], local.at[i]) for i in range(count)
    ]
    for copy in copies:
        copy.start()
    enter(rep, me, partners, False)
    for copy in copies:
        copy.wait()
    started = {}
    for tick in range(len(pieces) + depth - 1):
        for j in reversed(range(depth)):
            b = tick - j
            if not 0 <= b < len(pieces):
                continue
            if j > 0:
                started[b, j - 1].wait_recv()
            which, rows, cols = pieces[b]
            part = outs[which].at[(slice(None),) * j + tuple(bits[j:]) + (rows, cols)]
            copy = pltpu.make_async_remote_copy(
                part,
                part,
                send.at[b, j],
                recv.at[b, j],
                device_id=(rep, partners[j]),
                device_id_type=MESH,
            )
            copy.start()
            started[b, j] = copy
    for (b, j), copy in started.items():
        copy.wait_send()
        if j == depth - 1:
            copy.wait_recv()


def gather_all(n, shards, collective_id):
    depth = int(math.log2(n))
    pieces = []
    for i, shard in enumerate(shards):
        r, c = shard.shape
        if c > 512:
            pieces += [(i, slice(None), pl.ds(at, 512)) for at in range(0, c, 512)]
        elif r >= 128:
            pieces += [(i, pl.ds(at, 32), slice(None)) for at in range(0, r, 32)]
        else:
            pieces.append((i, slice(None), slice(None)))
    count = len(shards)
    outs = pl.pallas_call(
        functools.partial(gather_kernel, depth, pieces, count),
        out_shape=[jax.ShapeDtypeStruct((2,) * depth + s.shape, s.dtype) for s in shards],
        in_specs=[pl.BlockSpec(memory_space=pl.ANY)] * count,
        out_specs=[pl.BlockSpec(memory_space=pl.ANY)] * count,
        scratch_shapes=[
            pltpu.SemaphoreType.DMA((len(pieces), depth)),
            pltpu.SemaphoreType.DMA((len(pieces), depth)),
            pltpu.SemaphoreType.DMA((count,)),
        ],
        name="gather_weights",
        compiler_params=pltpu.CompilerParams(collective_id=collective_id, has_side_effects=True),
    )(*shards)
    return [out.reshape(n * s.shape[0], s.shape[1]) for out, s in zip(outs, shards)]


def scatter_kernel(depth, pieces, groups, count, *refs):
    ins, outs = refs[:count], refs[count : 2 * count]
    at = 2 * count
    stages = depth + 1
    gives = {}
    gets = {}
    for group in groups:
        gives[group] = refs[at : at + stages]
        gets[group] = refs[at + stages : at + 2 * stages]
        at += 2 * stages
    send, recv = refs[at:]
    rep, me = lax.axis_index("rep"), lax.axis_index("dp")
    bits = own_bits(me, depth)
    partners = [partner_of(me, bits[j], depth, j) for j in range(depth)]
    enter(rep, me, partners, True)
    started = {}
    for tick in range(len(pieces) + depth + 1):
        for s in reversed(range(depth + 2)):
            b = tick - s
            if not 0 <= b < len(pieces):
                continue
            which, rows, cols, group, slot = pieces[b]
            source = ins[which]
            j = depth - 1 - s
            if s > 0:
                started[b, s - 1].wait_recv()
            if s == depth + 1:
                mine = gives[group][depth][slot].astype(f32)
                outs[which][rows, cols] = mine + gets[group][depth][slot].astype(f32)
                continue
            if j >= 0:
                head = (slice(None),) * j
                tail = tuple(bits[j + 1 :]) + (rows, cols)
                give = head + (1 - bits[j],) + tail
                keep = head + (bits[j],) + tail
                if s == 0:
                    gives[group][0][slot] = source[give].astype(bf16)
                else:
                    got = gets[group][s - 1].at[slot]
                    gives[group][s][slot] = (
                        source[give] + got[head + (1 - bits[j],)].astype(f32)
                    ).astype(bf16)
                    source[keep] = source[keep] + got[head + (bits[j],)].astype(f32)
                target = (rep, partners[j])
            else:
                got = gets[group][s - 1][slot].astype(f32)
                gives[group][s][slot] = (source[tuple(bits) + (rows, cols)] + got).astype(bf16)
                target = (1 - rep, me)
            copy = pltpu.make_async_remote_copy(
                gives[group][s].at[slot],
                gets[group][s].at[slot],
                send.at[b, s],
                recv.at[b, s],
                device_id=target,
                device_id_type=MESH,
            )
            copy.start()
            started[b, s] = copy
    for copy in started.values():
        copy.wait_send()


def scatter_all(n, grads, collective_id):
    depth = int(math.log2(n))
    pieces, views, shapes, sizes = [], [], [], {}
    for i, grad in enumerate(grads):
        r, c = grad.shape[0] // n, grad.shape[1]
        views.append(grad.reshape((2,) * depth + (r, c)))
        shapes.append((r, c))
        high, wide = min(r, 32), min(c, 512)
        for a in range(0, r, high):
            for q in range(0, c, wide):
                slot = sizes.get((high, wide), 0)
                sizes[high, wide] = slot + 1
                pieces.append((i, pl.ds(a, high), pl.ds(q, wide), (high, wide), slot))
    count = len(grads)
    groups = sorted(sizes)
    scratch = []
    for group in groups:
        buffers = [
            VMEM((sizes[group],) + (2,) * max(depth - 1 - s, 0) + group, bf16)
            for s in range(depth + 1)
        ]
        scratch += buffers + buffers
    return pl.pallas_call(
        functools.partial(scatter_kernel, depth, pieces, groups, count),
        out_shape=[jax.ShapeDtypeStruct(s, f32) for s in shapes],
        in_specs=[pl.BlockSpec(memory_space=VMEM)] * count,
        out_specs=[pl.BlockSpec(memory_space=VMEM)] * count,
        scratch_shapes=scratch
        + [
            pltpu.SemaphoreType.DMA((len(pieces), depth + 1)),
            pltpu.SemaphoreType.DMA((len(pieces), depth + 1)),
        ],
        name="scatter_gradients",
        compiler_params=pltpu.CompilerParams(
            collective_id=collective_id, has_side_effects=True, vmem_limit_bytes=60 * 2**20
        ),
    )(*views)


def both_heads(pair, low):
    zero = jnp.zeros_like(pair)
    return jnp.concatenate([jnp.where(low, pair, zero), jnp.where(low, zero, pair)], axis=0)


def twice(bias):
    return bias if bias.shape[0] == 1 else jnp.concatenate([bias, bias], axis=0)


def attend_block(q, k, v, ctx, lse, rows, key_rows, keys, bias, size):
    low = lax.broadcasted_iota(jnp.int32, (size, 128), 1) < HD
    lanes = lax.broadcasted_iota(jnp.int32, (size, 128), 1)
    bias = twice(bias)
    log_sums = jnp.zeros((size, 128), f32)
    for pair in range(HEADS // 2):
        cols = pl.ds(128 * pair, 128)
        s = dot(both_heads(q[rows, cols], low), k[keys, cols], NT) * SCORE + bias
        largest = jnp.max(s, axis=1, keepdims=True)
        powers = jnp.exp2(s - largest)
        total = jnp.sum(powers, axis=1, keepdims=True)
        c = dot(powers.astype(bf16), v[keys, cols], NN) * (1.0 / total)
        ctx[rows, cols] = jnp.where(low, c[:size], c[size:]).astype(bf16)
        if lse is not None:
            log_sum = largest + jnp.log2(total)
            log_sums = jnp.where(lanes == 2 * pair, log_sum[:size], log_sums)
            log_sums = jnp.where(lanes == 2 * pair + 1, log_sum[size:], log_sums)
    if lse is not None:
        lse[key_rows, :] = log_sums


def column_pair(table, rows, pair):
    return jnp.concatenate(
        [table[rows, 2 * pair : 2 * pair + 1], table[rows, 2 * pair + 1 : 2 * pair + 2]], axis=0
    )


def attend_back_block(q, k, v, g, lse, delta, gq, gk_t, gv_t, rows, keys, bias, size):
    low = lax.broadcasted_iota(jnp.int32, (size, 128), 1) < HD
    bias = twice(bias)
    for pair in range(HEADS // 2):
        cols = pl.ds(128 * pair, 128)
        q_two = both_heads(q[rows, cols], low)
        g_two = both_heads(g[rows, cols], low)
        k_pair, v_pair = k[keys, cols], v[keys, cols]
        probs = jnp.exp2(dot(q_two, k_pair, NT) * SCORE + bias - column_pair(lse, rows, pair))
        grad_s = (probs * (dot(g_two, v_pair, NT) - column_pair(delta, rows, pair))).astype(bf16)
        gv_t[cols, keys] += dot(g_two, probs.astype(bf16), TN)
        gk_t[cols, keys] += dot(q_two, grad_s, TN)
        d = dot(grad_s, k_pair, NN)
        gq[rows, cols] = (jnp.where(low, d[:size], d[size:]) * SCALING).astype(bf16)


def head_sums(value):
    rows = value.shape[0]
    lanes = lax.broadcasted_iota(jnp.int32, (rows, 128), 1)
    low = lanes < HD
    result = jnp.zeros((rows, 128), f32)
    for pair in range(HEADS // 2):
        part = value[:, 128 * pair : 128 * pair + 128]
        first = jnp.sum(jnp.where(low, part, 0.0), axis=1, keepdims=True)
        second = jnp.sum(jnp.where(low, 0.0, part), axis=1, keepdims=True)
        result = jnp.where(lanes == 2 * pair, first, result)
        result = jnp.where(lanes == 2 * pair + 1, second, result)
    return result


def blocks(total, size, body):
    def step(i, carry):
        body(pl.ds(pl.multiple_of(i * size, size), size))
        return carry

    lax.fori_loop(0, total // size, step, 0)


def normalise(value):
    average = jnp.mean(value, axis=1, keepdims=True)
    centred = value - average
    scale = lax.rsqrt(jnp.mean(centred * centred, axis=1, keepdims=True) + EPSILON)
    return centred * scale, scale


def normalise_back(grad, gain, hat, scale):
    g = grad * gain
    first = jnp.mean(g, axis=1, keepdims=True)
    second = jnp.mean(g * hat, axis=1, keepdims=True)
    return scale * (g - first - hat * second)


def column_sum(value):
    return jnp.sum(value, axis=0, keepdims=True)


def prepare_kernel(
    x, t, mem, seg_c, seg_r, key_c, key_r, want_c, lang, wq, wk, wv, wck, wcv, small,
    h, q, k, v, ck, cv,
):
    length = x.shape[0]

    def glanced(rows):
        same = seg_c[rows, :] == seg_r[...]
        doc_length = jnp.sum(same.astype(f32), axis=1, keepdims=True)
        ahead = jnp.logical_and(same, key_r[...] > key_c[rows, :])
        rank = jnp.sum(ahead.astype(f32), axis=1, keepdims=True)
        wanted = jnp.minimum(want_c[rows, :], doc_length.astype(jnp.int32))
        count = lax.shift_right_logical(wanted + 1, jnp.int32(1))
        glance = rank < count.astype(f32)
        plain = x[rows, :].astype(f32)
        h[0, rows, :] = plain + lang[...]
        h[1, rows, :] = jnp.where(glance, t[rows, :].astype(f32), plain) + lang[...]

    blocks(length, 128, glanced)

    def cross(rows):
        m = mem[rows, :]
        ck[rows, :] = dot(m, wck[...], NT).astype(bf16)
        cv[rows, :] = (dot(m, wcv[...], NT) + small[4:5, :]).astype(bf16)

    blocks(mem.shape[0], 512, cross)
    for which in range(2):

        def project(rows):
            low = h[which, rows, :].astype(bf16)
            q[which, rows, :] = (dot(low, wq[...], NT) + small[0:1, :]).astype(bf16)
            k[which, rows, :] = dot(low, wk[...], NT).astype(bf16)
            v[which, rows, :] = (dot(low, wv[...], NT) + small[1:2, :]).astype(bf16)

        blocks(length, 512, project)


def windows(length):
    return [w for w in (256, 384, 512, 640) if w < length] + [length]


def windowed(starts, needs, i, length, body):
    need, begin = needs[i], starts[i]
    sizes = windows(length)
    for at, size in enumerate(sizes):
        fits = need <= size
        if at > 0:
            fits = jnp.logical_and(fits, need > sizes[at - 1])

        @pl.when(fits)
        def _():
            start = pl.multiple_of(jnp.minimum(begin, length - size), 128)
            body(pl.ds(start, size))


def self_kernel(starts, needs, q, k, v, seg_c, seg_r, ctx, lse):
    length = q.shape[1]
    size = 128

    def step(i, carry):
        rows = pl.ds(pl.multiple_of(i * size, size), size)

        def body(keys):
            bias = jnp.where(seg_c[rows, :] == seg_r[:, keys], 0.0, MASKED)
            for which in range(2):
                attend_block(
                    q.at[which], k.at[which], v.at[which], ctx.at[which],
                    lse if which == 1 else None, rows, rows, keys, bias, size,
                )

        windowed(starts, needs, i, length, body)
        return carry

    lax.fori_loop(0, length // size, step, 0)


def after_self(ctx, h, wso, wcq, small, a, cq, rows):
    r1 = h + dot(ctx, wso[...], NT) + small[2:3, :]
    hat, scale = normalise(r1)
    value = hat * small[10:11, :] + small[7:8, :]
    a[rows, :] = value
    low = value.astype(bf16)
    cq[rows, :] = (dot(low, wcq[...], NT) + small[3:4, :]).astype(bf16)
    return hat, scale, low


def after_cross(a, ctx2, wco, win, wout, small, hidden_bias, hid, slope, rows):
    r2 = a[rows, :] + dot(ctx2[rows, :], wco[...], NT) + small[5:6, :]
    hat2, scale2 = normalise(r2)
    b = hat2 * small[11:12, :] + small[8:9, :]
    low = b.astype(bf16)
    total = b + small[6:7, :]
    for j in range(win.shape[0] // 512):
        cols = pl.ds(512 * j, 512)
        z = dot(low, win[cols, :], NT) + hidden_bias[:, cols]
        half = 0.5 + 0.5 * lax.erf(z * 0.7071067811865476)
        hidden = (z * half).astype(bf16)
        if hid is not None:
            hid[:, cols] = hidden
            bell = jnp.exp2(z * z * (-0.5 * LOG2E)) * 0.3989422804014327
            slope[:, cols] = half + z * bell
        total = total + dot(hidden, wout[:, cols], NT)
    hat3, scale3 = normalise(total)
    y = hat3 * small[12:13, :] + small[9:10, :]
    return y, (hat2, scale2, low, hat3, scale3)


def first_kernel(
    h, ctx, ck, cv, source_bias, wso, wcq, wco, win, wout, small, hidden_bias,
    out, a, cq, ctx2,
):
    length = h.shape[1]

    def before(rows):
        after_self(ctx[0, rows, :], h[0, rows, :], wso, wcq, small, a, cq, rows)

    blocks(length, 512, before)
    every = pl.ds(0, ck.shape[0])
    blocks(
        length,
        256,
        lambda rows: attend_block(cq, ck, cv, ctx2, None, rows, rows, every, source_bias[...], 256),
    )

    def last(rows):
        y, _ = after_cross(a, ctx2, wco, win, wout, small, hidden_bias, None, None, rows)
        out[rows, :] = y.astype(bf16)

    blocks(length, 512, last)


def layer_kernel(
    h, ctx, ck, cv, mem, cot, live, source_bias,
    wso, wcq, wck, wcv, wco, win, wout, small, hidden_bias,
    out, gr1, gctx, g_mem,
    g_so, g_cq, g_ck, g_cv, g_co, g_in, g_out, g_small, g_hidden,
    cq, ctx2, lse2, hat1, scale1, low1, hid, slope, delta, gcq, gk_low, gv_low, low2, hat2s,
):
    length = h.shape[1]
    big = 512
    a, gctx2 = gr1, gctx
    for ref in (g_so, g_cq, g_co, g_in, g_out, g_small, g_hidden):
        ref[...] = jnp.zeros_like(ref)

    def before(rows):
        hat, scale, low = after_self(ctx[0, rows, :], h[0, rows, :], wso, wcq, small, a, cq, rows)
        hat1[rows, :] = hat
        scale1[rows, :] = scale
        low1[rows, :] = low

    blocks(length, big, before)
    every = pl.ds(0, ck.shape[0])
    blocks(
        length,
        256,
        lambda rows: attend_block(cq, ck, cv, ctx2, lse2, rows, rows, every, source_bias[...], 256),
    )

    def turn(rows):
        y, (hat2, scale2, low, hat3, scale3) = after_cross(
            a, ctx2, wco, win, wout, small, hidden_bias, hid, slope, rows
        )
        out[rows, :] = y.astype(bf16)
        low2[...] = low
        hat2s[...] = hat2
        gy = cot[rows, :].astype(f32) * live[rows, :]
        g_small[12:13, :] += column_sum(gy * hat3)
        g_small[9:10, :] += column_sum(gy)
        gr3 = normalise_back(gy, small[12:13, :], hat3, scale3)
        gf = gr3.astype(bf16)
        g_small[6:7, :] += column_sum(gf.astype(f32))
        gb = gr3
        for j in range(win.shape[0] // 512):
            cols = pl.ds(512 * j, 512)
            gz = (dot(gf, wout[:, cols], NN) * slope[:, cols]).astype(bf16)
            g_out[:, cols] += dot(gf, hid[:, cols], TN)
            g_in[cols, :] += dot(gz, low2[...], TN)
            g_hidden[:, cols] += column_sum(gz.astype(f32))
            gb = gb + dot(gz, win[cols, :], NN)
        hat2 = hat2s[...]
        g_small[11:12, :] += column_sum(gb * hat2)
        g_small[8:9, :] += column_sum(gb)
        gr2 = normalise_back(gb, small[11:12, :], hat2, scale2)
        a[rows, :] = gr2
        go2 = gr2.astype(bf16)
        g_small[5:6, :] += column_sum(go2.astype(f32))
        context = ctx2[rows, :]
        g_co[...] += dot(go2, context, TN)
        back = dot(go2, wco[...], NN).astype(bf16)
        gctx2[rows, :] = back
        delta[rows, :] = head_sums(back.astype(f32) * context.astype(f32))

    blocks(length, big, turn)
    gk_t, gv_t = slope.at[:, pl.ds(0, ck.shape[0])], slope.at[:, pl.ds(ck.shape[0], ck.shape[0])]
    slope[...] = jnp.zeros_like(slope)
    blocks(
        length,
        256,
        lambda rows: attend_back_block(
            cq, ck, cv, gctx2, lse2, delta, gcq, gk_t, gv_t, rows, every, source_bias[...], 256
        ),
    )
    gk_low[...] = (gk_t[...] * SCALING).astype(bf16)
    gv_low[...] = gv_t[...].astype(bf16)
    g_ck[...] = dot(gk_low[...], mem[...], NN)
    g_cv[...] = dot(gv_low[...], mem[...], NN)
    ones = jnp.ones((8, mem.shape[0]), bf16)
    g_small[4:5, :] = dot(ones, gv_low[...], NT)[0:1, :]
    for at in range(0, mem.shape[0], 512):
        cols = pl.ds(at, 512)
        g_mem[cols, :] = dot(gk_low[:, cols], wck[...], TN) + dot(gv_low[:, cols], wcv[...], TN)

    def final(rows):
        gq = gcq[rows, :]
        g_small[3:4, :] += column_sum(gq.astype(f32))
        g_cq[...] += dot(gq, low1[rows, :], TN)
        ga = a[rows, :] + dot(gq, wcq[...], NN)
        hat = hat1[rows, :]
        g_small[10:11, :] += column_sum(ga * hat)
        g_small[7:8, :] += column_sum(ga)
        g1 = normalise_back(ga, small[10:11, :], hat, scale1[rows, :])
        gr1[rows, :] = g1
        go = g1.astype(bf16)
        g_small[2:3, :] += column_sum(go.astype(f32))
        g_so[...] += dot(go, ctx[0, rows, :], TN)
        gctx[rows, :] = dot(go, wso[...], NN).astype(bf16)

    blocks(length, big, final)


def self_back_kernel(
    starts, needs, live_blocks, q, k, v, g, ctx, lse, seg_c, seg_r,
    gq, gk_low, gv_low, delta, gk_t, gv_t,
):
    length = q.shape[1]
    size = 128
    gk_t[...] = jnp.zeros_like(gk_t)
    gv_t[...] = jnp.zeros_like(gv_t)
    gq[...] = jnp.zeros_like(gq)

    def step(i, carry):
        rows = pl.ds(pl.multiple_of(i * size, size), size)
        delta[rows, :] = head_sums(g[rows, :].astype(f32) * ctx[0, rows, :].astype(f32))

        def body(keys):
            bias = jnp.where(seg_c[rows, :] == seg_r[:, keys], 0.0, MASKED)
            attend_back_block(
                q.at[0], k.at[0], v.at[0], g, lse, delta, gq, gk_t, gv_t, rows, keys, bias, size
            )

        windowed(starts, needs, i, length, body)
        return carry

    lax.fori_loop(0, live_blocks[0], step, 0)
    gk_low[...] = (gk_t[...] * SCALING).astype(bf16)
    gv_low[...] = gv_t[...].astype(bf16)


def input_kernel(h, gq, gk_low, gv_low, gr1, wq, wk, wv, g_x, g_q, g_k, g_v, sums):
    length = h.shape[1]
    g_q[...] = jnp.zeros_like(g_q)
    g_k[...] = jnp.zeros_like(g_k)
    g_v[...] = jnp.zeros_like(g_v)
    sums[...] = jnp.zeros_like(sums)
    ones = jnp.ones((8, 512), bf16)

    for at in range(0, length, 512):
        rows = pl.ds(at, 512)
        low = h[0, rows, :].astype(bf16)
        part = gq[rows, :]
        g_q[...] += dot(part, low, TN)
        g_k[...] += dot(gk_low[:, rows], low, NN)
        g_v[...] += dot(gv_low[:, rows], low, NN)
        value = gr1[rows, :] + dot(part, wq[...], NN)
        value = value + dot(gk_low[:, rows], wk[...], TN) + dot(gv_low[:, rows], wv[...], TN)
        g_x[rows, :] = value
        sums[0:1, :] += column_sum(part.astype(f32))
        sums[1:2, :] += dot(ones, gv_low[:, rows], NT)[0:1, :]
        sums[2:3, :] += column_sum(value)


def shape(dims, dtype=f32):
    return jax.ShapeDtypeStruct(dims, dtype)


def call(kernel, name, outs, args, scratch=(), scalars=0, specs=None):
    in_specs = [pl.BlockSpec(memory_space=pltpu.SMEM)] * scalars
    for at in range(scalars, len(args)):
        in_specs.append((specs or {}).get(at) or pl.BlockSpec(memory_space=VMEM))
    return pl.pallas_call(
        kernel,
        out_shape=outs,
        in_specs=in_specs,
        out_specs=[pl.BlockSpec(memory_space=VMEM)] * len(outs),
        scratch_shapes=list(scratch),
        name=name,
        compiler_params=pltpu.CompilerParams(vmem_limit_bytes=61 * 2**20),
    )(*args)


def shards(
    n,
    x_copy,
    target_embed,
    memory,
    cotangent,
    segment_ids,
    source_lengths,
    target_lengths,
    hamming,
    priority,
    lang_tag,
    w_self_qkv,
    w_self_out,
    w_cross_q,
    w_cross_kv,
    w_cross_out,
    w_in,
    w_out,
    biases,
    gains,
    b_hidden,
    lang_table,
):
    length, width = x_copy.shape[1:]
    source = memory.shape[1]
    hidden = b_hidden.shape[0] * n
    share = width // n
    fold = hidden // width
    langs = lang_table.shape[0]
    slots = hamming.shape[1]

    table = jnp.concatenate([biases, gains, lang_table, b_hidden.reshape(fold, share)], axis=0)
    kept = table.shape[0]
    table = jnp.pad(table, ((0, 128 - kept), (0, 0)))
    gathered = gather_all(
        n,
        [
            table.T,
            w_cross_kv[0].T,
            w_cross_kv[1].T,
            w_self_qkv[0].T,
            w_self_qkv[1].T,
            w_self_qkv[2].T,
            w_self_out.T,
            w_cross_q.T,
            w_cross_out.T,
            w_in.T,
            w_out.T,
        ],
        0,
    )
    small_t, wck, wcv, wq, wk, wv, wso, wcq, wco, win, wout = gathered
    small = small_t.T.astype(f32)
    first_lang = BIASES + GAINS
    hidden_bias = small[first_lang + langs : first_lang + langs + fold]
    hidden_bias = hidden_bias.reshape(fold, n, share).transpose(1, 0, 2).reshape(1, hidden)
    lang = lax.dynamic_slice_in_dim(small, first_lang + lang_tag[0], 1, 0)
    small = small[:16]

    target_len = target_lengths[0]
    position = jnp.arange(length, dtype=jnp.int32)
    live = position < target_len
    seg = jnp.where(live, segment_ids[0], slots).astype(jnp.int32)
    wanted = jnp.sum(
        jnp.where(seg[:, None] == jnp.arange(slots, dtype=jnp.int32)[None, :], hamming[0][None, :], 0),
        axis=1,
        keepdims=True,
    )
    key = priority[0] * length + (length - 1 - position)
    same_edge = seg.reshape(length // 128, 128)
    first_seg, last_seg = same_edge[:, 0], same_edge[:, -1]
    begin = jnp.sum((seg[None, :] < first_seg[:, None]).astype(jnp.int32), axis=1)
    end = jnp.sum((seg[None, :] <= last_seg[:, None]).astype(jnp.int32), axis=1)
    starts = begin // 128 * 128
    needs = (end + 127) // 128 * 128 - starts
    live_blocks = ((target_len + 127) // 128).reshape(1)
    seg_c, seg_r = seg[:, None], seg[None, :]
    source_bias = jnp.where(
        jnp.arange(source, dtype=jnp.int32) < source_lengths[0], 0.0, MASKED
    ).astype(f32)[None, :]

    mem = memory[0]
    two = (2, length, width)
    h, q, k, v, ck, cv = call(
        prepare_kernel,
        "prepare",
        [shape(two), shape(two, bf16), shape(two, bf16), shape(two, bf16)]
        + [shape((source, width), bf16)] * 2,
        (
            x_copy[0], target_embed[0], mem, seg_c, seg_r, key[:, None], key[None, :], wanted,
            lang, wq, wk, wv, wck, wcv, small,
        ),
    )
    ctx, lse = call(
        self_kernel,
        "self_attention",
        [shape(two, bf16), shape((length, 128))],
        (starts, needs, q, k, v, seg_c, seg_r),
        scalars=2,
    )

    def part(dims, which):
        block = (1,) + dims[1:]
        return pl.BlockSpec(block, lambda i: (which, 0, 0))

    def one(value, which):
        return lax.slice_in_dim(value, which, which + 1, axis=0)

    flat = (length, width)
    (first,) = call(
        first_kernel,
        "first_pass",
        [shape(flat, bf16)],
        (one(h, 0), one(ctx, 0), ck, cv, source_bias, wso, wcq, wco, win, wout, small, hidden_bias),
        scratch=[VMEM(flat, f32), VMEM(flat, bf16), VMEM(flat, bf16)],
    )
    square = shape((width, width))
    h2, ctx_two = one(h, 1), one(ctx, 1)
    big = 512
    (
        final, gr1, gctx, g_mem, g_so, g_cq, g_ck, g_cv, g_co, g_in, g_out, g_small, g_hidden,
    ) = call(
        layer_kernel,
        "second_pass",
        [shape(flat, bf16), shape(flat), shape(flat, bf16), shape((source, width))]
        + [square] * 5
        + [shape((hidden, width)), shape((width, hidden)), shape((16, width)), shape((1, hidden))],
        (
            h2, ctx_two, ck, cv, mem, cotangent[0], live[:, None].astype(f32), source_bias,
            wso, wcq, wck, wcv, wco, win, wout, small, hidden_bias,
        ),
        scratch=[
            VMEM(flat, bf16), VMEM(flat, bf16), VMEM((length, 128), f32),
            VMEM(flat, f32), VMEM((length, 1), f32), VMEM(flat, bf16),
            VMEM((big, hidden), bf16), VMEM((width, max(hidden, 2 * source)), f32),
            VMEM((length, 128), f32), VMEM(flat, bf16),
            VMEM((width, source), bf16), VMEM((width, source), bf16),
            VMEM((big, width), bf16), VMEM((big, width), f32),
        ],
    )
    gq, gk_low, gv_low = call(
        self_back_kernel,
        "self_attention_back",
        [shape(flat, bf16), shape((width, length), bf16), shape((width, length), bf16)],
        (starts, needs, live_blocks, one(q, 1), one(k, 1), one(v, 1), gctx, ctx_two, lse, seg_c, seg_r),
        scratch=[VMEM((length, 128), f32), VMEM((width, length), f32), VMEM((width, length), f32)],
        scalars=3,
    )
    g_x, g_q, g_k, g_v, sums = call(
        input_kernel,
        "input_gradient",
        [shape(flat), square, square, square, shape((8, width))],
        (h2, gq, gk_low, gv_low, gr1, wq, wk, wv),
    )

    tag = jnp.arange(langs, dtype=jnp.int32) == lang_tag[0]
    g_lang = jnp.where(tag[:, None], sums[2:3], 0.0)
    g_fold = g_hidden.reshape(n, fold, share).transpose(1, 0, 2).reshape(fold, width)
    g_table = jnp.concatenate([sums[0:2], g_small[2:13], g_lang, g_fold], axis=0)
    g_table = jnp.pad(g_table, ((0, 128 - kept), (0, 0))).T
    owned = scatter_all(n, [g_in, g_out, g_co, g_ck, g_cv, g_cq, g_so, g_q, g_k, g_v, g_table], 1)
    o_in, o_out, o_co, o_ck, o_cv, o_cq, o_so, o_q, o_k, o_v, o_table = owned
    o_table = o_table.T
    return (
        first[None],
        final[None],
        g_x[None],
        g_mem[None],
        jnp.stack([o_q.T, o_k.T, o_v.T]),
        o_so.T,
        o_cq.T,
        jnp.stack([o_ck.T, o_cv.T]),
        o_co.T,
        o_in.T,
        o_out.T,
        o_table[:BIASES],
        o_table[BIASES:first_lang],
        o_table[first_lang + langs : kept].reshape(hidden // n),
        o_table[first_lang : first_lang + langs],
    )


def solution(mesh):
    n = mesh.shape["dp"]
    row3, row2, row1 = P(("rep", "dp"), None, None), P(("rep", "dp"), None), P(("rep", "dp"))
    wide, tall, flat = P(None, None, "dp"), P(None, "dp"), P("dp")
    parameters = (wide, tall, tall, wide, tall, tall, tall, tall, tall, flat, tall)
    return jax.shard_map(
        functools.partial(shards, n),
        mesh=mesh,
        in_specs=(row3, row3, row3, row3, row2, row1, row1, row2, row2, row1) + parameters,
        out_specs=(row3, row3, row3, row3) + parameters,
        check_vma=False,
    )
```

time: 1210 us -> 436 us (0.36)
  waiting for transfers between devices: 399 us -> 0 us
  Pallas kernels: 0 us -> 375 us
  matrix products: 372 us -> 0 us
  blocking collectives: 246 us -> 0 us
  other arithmetic: 127 us -> 13.9 us
  between operations: 19.4 us -> 3.3 us
    pallas_call x0 -> x8, Pallas kernels: none -> 375 us  [the longest x6 165 us: call(): pl.pallas_call(kernel, out_shape=outs, in_specs=in_specs, out_specs=[pl.B...]
    reduce_scatter x7 -> x0, waiting for transfers between devices: 365 us -> none  [the longest x1 74.5 us: shards(): lax.psum_scatter(local_grads[5], 'dp', scatter_dimension=1, tiled=True)]
    dot_general x66 -> x0, matrix products: 331 us -> none  [the longest x18 76.3 us: product(): return jnp.dot(left, right, preferred_element_type=jnp.float32)]
    all_gather x7 -> x0, blocking collectives: 145 us -> none  [the longest x1 23.4 us: shards(): lax.all_gather(w_cross_out, 'dp', axis=1, tiled=True)]
    unnamed x1 -> x0, blocking collectives: 101 us -> none
    convert_element_type x26 -> x2, other arithmetic: 73.9 us -> 1.78 us  [the longest x1 0.92 us: shards(): small = small_t.T.astype(f32)]
    reduce_sum x20 -> x2, other arithmetic: 43.1 us -> 0.95 us  [the longest x1 0.73 us: shards(): jnp.sum(jnp.where(seg[:, None] == jnp.arange(slots, dtype=jnp.int32)[None...]
    sub x4 -> x0, matrix products: 41 us -> none  [attend(): powers = jnp.exp(scores - largest)]
  transfers between devices with their start and end apart: 15 -> 0, of which waited for: 8 -> 0; matrix products, arithmetic and copies ran while one was open for 26% -> 0% of each run, Pallas kernels for 0% -> 0%
where the time goes in v1:
time: 436 us; the launch traced here: 430 us
  Pallas kernels  375 us (86%)
  local copies, waits for them, and re-layouts  37.4 us (9%)
  other arithmetic  13.9 us (3%)
    pallas_call x6, Pallas kernels, call(): pl.pallas_call(kernel, out_shape=outs, in_specs=in_specs, out_specs=[pl.B...  165 us
    pallas_call x1, Pallas kernels, gather_all(): pl.pallas_call(functools.partial(gather_kernel, depth, pieces, count), ou...  110 us
    pallas_call x1, Pallas kernels, scatter_all(): pl.pallas_call(functools.partial(scatter_kernel, depth, pieces, groups, c...  100 us
    unnamed x26, local copies, waits for them, and re-layouts  14 us
    slice x5, local copies, waits for them, and re-layouts, one(): return lax.slice_in_dim(value, which, which + 1, axis=0)  9.43 us

profile of v1, /device:TPU:0, one launch (start us, length us, event | category | flops | bytes accessed | tf_op | source)
XLA Modules:
  0.0 429.7 jit_solution(6340305995089539992)
XLA Ops:
  7.8 1.4 fusion.10.refs_0_
  9.2 1.3 subtract_add_fusion.1
  12.0 1.7 copy.107
  13.7 1.5 slice_bitcast_fusion
  18.6 110.0 %gather_weights.1 = (bf16[2,2,2,2,32,128]{5,4,3,2,1,0:T(8,128)(2,1)}, bf16[2,2,2,2,32,512]{5,4,3,2,1,0:T(8,128)(2,1)}, bf16[2,2,2,2,32,512]{5,4,3,2,1,0:T(8,128)...) custom-call(bf16[32,128]{1,0:T(8,128)(2,1)} %fusion.10.refs_0_, ...), custom_call_target="tpu_custom_call" | custom-call | tf_op jit(solution)/shard_map/gather_weights/pallas_call | solution.py:103
  132.8 15.0 %prepare.1 = (f32[2,1024,512]{2,1,0:T(8,128)}, bf16[2,1024,512]{2,1,0:T(8,128)(2,1)}, bf16[2,1024,512]{2,1,0:T(8,128)(2,1)}, bf16[2,1024,512]{2,1,0:T(8,128)(2,1...) custom-call(bf16[1024,512]{1,0:T(8,128)(2,1)} %bitcast.141, bf16[1024,512]{1,0:T(8,128)(2,1)} %bitcast.142, ...), custom_call_target="tpu_custom_call" | custom-call | tf_op jit(solution)/shard_map/prepare/pallas_call | solution.py:601
  147.8 4.8 %fusion.14 = (f32[1,1024,512]{2,1,0:T(8,128)}, f32[1,1024,512]{2,1,0:T(8,128)}) fusion(f32[2,1024,512]{2,1,0:T(8,128)} %get-tuple-element.72), kind=kLoop, calls=%fused_computation.52 | loop fusion | bytes 8388608 | tf_op jit(solution)/shard_map/slice | solution.py:719
  153.7 24.8 %self_attention.1 = (bf16[2,1024,512]{2,1,0:T(8,128)(2,1)}, f32[1024,128]{1,0:T(8,128)}) custom-call(s32[8]{0:T(128)} %get-tuple-element.195.starts, s32[8]{0:T(128)} %get-tuple-element.194.needs, bf16[2,1024,512]{2,1,0:T(8,128)(2,1)} %get-tuple-element.73.q, bf16[2,1024,512]{2,1,0:T(8,128)(2,1)} %get-tuple-element.74.k, ...), custom_call_target="tpu_custom_call" | custom-call | tf_op jit(solution)/shard_map/self_attention/pallas_call | solution.py:601
  178.5 1.1 slice.84.v
  181.5 1.4 fusion.15
  183.0 27.8 %first_pass.1 = bf16[1024,512]{1,0:T(8,128)(2,1)} custom-call(f32[1,1024,512]{2,1,0:T(8,128)} %get-tuple-element.197.h, bf16[1,1024,512]{2,1,0:T(8,128)(2,1)} %get-tuple-element.199.ctx, bf16[1024,512]{1,0:T(8,128)(2,1)} %get-tuple-element.77.ck, bf16[1024,512]{1,0:T(8,128)(2,1)} %get-tuple-element.78.cv, f32[1,1024]{1,0:T(1,128)} %compare_select_fusion.source_bias, ...), custom_call_target="tpu_custom_call" | custom-call | tf_op jit(solution)/shard_map/first_pass/pallas_call | solution.py:601
  210.8 74.4 %second_pass.1 = (bf16[1024,512]{1,0:T(8,128)(2,1)}, f32[1024,512]{1,0:T(8,128)}, bf16[1024,512]{1,0:T(8,128)(2,1)}, f32[1024,512]{1,0:T(8,128)}, f32[512,512]{1...) custom-call(f32[1,1024,512]{2,1,0:T(8,128)} %get-tuple-element.196.h, ...), custom_call_target="tpu_custom_call" | custom-call | tf_op jit(solution)/shard_map/second_pass/pallas_call | solution.py:601
  285.2 14.5 %self_attention_back.1 = (bf16[1024,512]{1,0:T(8,128)(2,1)}, bf16[512,1024]{1,0:T(8,128)(2,1)}, bf16[512,1024]{1,0:T(8,128)(2,1)}) custom-call(s32[8]{0:T(128)} %get-tuple-element.195.starts, s32[8]{0:T(128)} %get-tuple-element.194.needs, s32[1]{0:T(128)} %bitcast.48.live_blocks, bf16[1,1024,512]{2,1,0:T(8,128)(2,1)} %slice.82.q, ...), custom_call_target="tpu_custom_call" | custom-call | tf_op jit(solution)/shard_map/self_attention_back/pallas_call | solution.py:601
  299.7 8.5 %input_gradient.1 = (f32[1024,512]{1,0:T(8,128)}, f32[512,512]{1,0:T(8,128)}, f32[512,512]{1,0:T(8,128)}, f32[512,512]{1,0:T(8,128)}, f32[8,512]{1,0:T(8,128)}) custom-call(f32[1,1024,512]{2,1,0:T(8,128)} %get-tuple-element.196.h, bf16[1024,512]{1,0:T(8,128)(2,1)} %get-tuple-element.87.gq, bf16[512,1024]{1,0:T(8,128)(2,1)} %get-tuple-element.88.gk_low, ...), custom_call_target="tpu_custom_call" | custom-call | tf_op jit(solution)/shard_map/input_gradient/pallas_call | solution.py:601
  312.5 100.0 %scatter_gradients.1 = (f32[128,512]{1,0:T(8,128)}, f32[32,2048]{1,0:T(8,128)}, f32[32,512]{1,0:T(8,128)}, f32[32,512]{1,0:T(8,128)}, f32[32,512]{1,0:T(8,128)},...) custom-call(f32[2,2,2,2,128,512]{5,4,3,2,1,0:T(8,128)} %bitcast.120,, ...), custom_call_target="tpu_custom_call" | custom-call | tf_op jit(solution)/shard_map/scatter_gradients/pallas_call | solution.py:203
  412.5 1.6 pad_maximum_fusion
  414.1 1.4 copy.117
  415.5 1.4 slice.99
  419.8 1.5 pad_maximum_fusion.1
  421.3 1.8 copy.116
  423.1 1.5 copy.128
  424.6 1.5 copy.129
  426.1 1.5 copy.130
  427.5 1.7 copy.131
  (61 shorter events, 24.5 us)
Async XLA Ops:
  0.6 15.8 %copy-start.5 = (s32[1,1024]{1,0:T(1,128)S(1)}, s32[1,1024]{1,0:T(1,128)}, u32[]{:S(2)}) copy-start(s32[1,1024]{1,0:T(1,128)} %param.25) | copy-start | bytes 12292
  4.7 13.0 %copy-start.4 = (s32[1,1024]{1,0:T(1,128)}, s32[1,1024]{1,0:T(1,128)S(1)}, u32[]{:S(2)}) copy-start(s32[1,1024]{1,0:T(1,128)S(1)} %compare_select_fusion.1.seg_r) | copy-start | bytes 12292
  147.8 4.8 %copy-start.2 = (bf16[2,1024,512]{2,1,0:T(8,128)(2,1)S(1)}, bf16[2,1024,512]{2,1,0:T(8,128)(2,1)}, u32[]{:S(2)}) copy-start(bf16[2,1024,512]{2,1,0:T(8,128)(2,1)} %get-tuple-element.73.q) | copy-start | bytes 6291460
  153.7 24.8 %copy-start.1 = (bf16[2,1024,512]{2,1,0:T(8,128)(2,1)S(1)}, bf16[2,1024,512]{2,1,0:T(8,128)(2,1)}, u32[]{:S(2)}) copy-start(bf16[2,1024,512]{2,1,0:T(8,128)(2,1)} %get-tuple-element.75.v) | copy-start | bytes 6291460
  178.5 2.0 copy-start
  178.5 3.0 copy-start.3
  299.7 10.4 %copy-start.7 = (f32[1,2048]{1,0:T(1,128)S(1)}, f32[1,2048]{1,0:T(1,128)}, u32[]{:S(2)}) copy-start(f32[1,2048]{1,0:T(1,128)} %get-tuple-element.105) | copy-start | bytes 24580
  299.7 11.2 %copy-start.6 = (f32[16,512]{1,0:T(8,128)S(1)}, f32[16,512]{1,0:T(8,128)}, u32[]{:S(2)}) copy-start(f32[16,512]{1,0:T(8,128)} %get-tuple-element.104) | copy-start | bytes 98308
